TPU v7x, 256 devices: a whole 4x4x8 slice. The times are simulated.
256 devices in a mesh: dp: 16 (over z_hi, y, core), tensor: 16 (over x, z_lo).
Axes of the slice: x: 4, y: 4, z: 8 (z_hi: 2, z_lo: 4; z = z_hi * 4 + z_lo), core: 2. Of those that a mesh axis runs over, the one named last changes fastest.
Arguments:
- residual_rows: bfloat16 [6144, 4096], P(('dp', 'tensor')), parts along dimension 0, may hold values from -6 to 6
- pending: bfloat16 [16, 6144, 4096], P('tensor', 'dp'), parts along dimension 1, may hold values from -1.5 to 1.5
- query_weight: bfloat16 [4096, 8192], P(None, 'tensor'), may hold values from -32 to 32
- key_weight: bfloat16 [4096, 1024], P(None, 'tensor'), may hold values from -32 to 32
- value_weight: bfloat16 [4096, 1024], P(None, 'tensor'), may hold values from -0.09375 to 0.09375
- out_weight: bfloat16 [8192, 4096], P('tensor'), may hold values from -0.25 to 0.25
- prompt_length: int32 [16], P('dp'), parts along dimension 0, may hold values from 96 to 384
Outputs:
- mixed: bfloat16 [6144, 4096], P(('dp', 'tensor')), parts along dimension 0
There are 16 independent parts, one for each index of `dp`. A program takes and returns all parts, laid end to end along the dimension named above; an argument that names none is the same for every part. Nothing has to cross between parts.
All inputs are finite; a program needn't handle non-finite values.
Results may differ from a plain program's by a relative error of at most 0.017.
The roundings to bfloat16 on the way count: a program that leaves them out, or rounds other values in their place, can miss the bound.
Values may be sent and summed in bfloat16 or wider, within the bound.
A program may use at most 64 MiB of HBM per device.

v0:
```python
import jax
import jax.numpy as jnp
from jax import lax
from jax.sharding import PartitionSpec as P

rope_base = 500000.0
norm_eps = 1e-05


def partner(value, axis, apart):
    return lax.ppermute(value, axis, [(i, i ^ 1 << apart) for i in range(lax.axis_size(axis))])


def rotate_pairs(stacked, positions):
    half_dim = stacked.shape[-1] // 2
    frequency = rope_base ** (-jnp.arange(half_dim, dtype=jnp.float32) * (2.0 / stacked.shape[-1]))
    angles = positions[:, None] * frequency[None, :]
    cosine = jnp.cos(angles)[:, None, :]
    sine_part = jnp.sin(angles)[:, None, :]
    first = stacked[..., :half_dim]
    second = stacked[..., half_dim:]
    return jnp.concatenate(
        [first * cosine - second * sine_part, second * cosine + first * sine_part], axis=-1
    )


def join_halves(own_part, other_part, parity):
    return jnp.where(
        parity == 0,
        jnp.concatenate([own_part, other_part], axis=1),
        jnp.concatenate([other_part, own_part], axis=1),
    )


def per_device(
    residual_rows, pending, query_weight, key_weight, value_weight, out_weight, prompt_length
):
    residual = residual_rows.astype(jnp.float32)
    normed_shard = (
        residual * lax.rsqrt(jnp.mean(residual * residual, axis=-1, keepdims=True) + norm_eps)
    ).astype(jnp.bfloat16)
    pending_total = lax.psum_scatter(
        pending[0].astype(jnp.float32).astype(jnp.bfloat16),
        "tensor",
        scatter_dimension=0,
        tiled=True,
    ).astype(jnp.float32)
    parity = lax.axis_index("tensor") % 2
    query_width = query_weight.shape[1]
    key_width = key_weight.shape[1]
    piece = lax.all_gather(normed_shard, "tensor", axis=0, tiled=True)
    projected = jnp.concatenate(
        [
            jnp.dot(piece, query_weight, preferred_element_type=jnp.float32),
            jnp.dot(piece, key_weight, preferred_element_type=jnp.float32),
            jnp.dot(piece, value_weight, preferred_element_type=jnp.float32),
        ],
        axis=1,
    )
    row_count = projected.shape[0]
    key_raw = projected[:, query_width : query_width + key_width].astype(jnp.bfloat16)
    value_rows = projected[:, query_width + key_width :].astype(jnp.bfloat16)
    other_key, other_value = partner((key_raw, value_rows), "tensor", 0)
    key_raw = join_halves(key_raw, other_key, parity)
    value_rows = join_halves(value_rows, other_value, parity)
    head_dim = key_raw.shape[1]
    heads_here = query_width // head_dim
    positions = jnp.arange(row_count, dtype=jnp.float32)
    query_rows = rotate_pairs(
        projected[:, :query_width].reshape(row_count, heads_here, head_dim), positions
    ).astype(jnp.bfloat16)
    key_rows = rotate_pairs(key_raw.astype(jnp.float32)[:, None, :], positions)[:, 0, :].astype(
        jnp.bfloat16
    )
    scores = jnp.einsum(
        "qhd,sd->hqs", query_rows, key_rows, preferred_element_type=jnp.float32
    ) * head_dim ** (-0.5)
    row_index = jnp.arange(row_count, dtype=jnp.int32)[:, None]
    col_index = jnp.arange(row_count, dtype=jnp.int32)[None, :]
    allowed = (col_index <= row_index) & (col_index < prompt_length[0])
    scores = jnp.where(allowed[None], scores, -1e30)
    largest = jnp.max(scores, axis=-1, keepdims=True)
    expo = jnp.exp(scores - largest)
    weights_soft = (expo / jnp.sum(expo, axis=-1, keepdims=True)).astype(jnp.bfloat16)
    attended = jnp.einsum(
        "hqs,sd->qhd", weights_soft, value_rows, preferred_element_type=jnp.float32
    )
    attended = attended.astype(jnp.bfloat16).reshape(row_count, query_width)
    total = (
        residual
        + pending_total
        + lax.psum_scatter(
            jnp.dot(attended, out_weight, preferred_element_type=jnp.float32),
            "tensor",
            scatter_dimension=0,
            tiled=True,
        )
    )
    return total.astype(jnp.bfloat16)


def solution(mesh):
    placed = (
        P(("dp", "tensor"), None),
        P("tensor", "dp", None),
        P(None, "tensor"),
        P(None, "tensor"),
        P(None, "tensor"),
        P("tensor", None),
        P("dp"),
    )
    return jax.shard_map(
        per_device, mesh=mesh, in_specs=placed, out_specs=P(("dp", "tensor"), None), check_vma=False
    )
```

profile of v0, /device:TPU:16, one launch (start us, length us, event | category | flops | bytes accessed | tf_op | source)
XLA Modules:
  0.0 352.5 jit_solution(7924590568680131958)
XLA Ops:
  6.5 0.0 copy-start
  6.5 0.0 all-gather.2.cloned.1.call-start
  6.5 1.1 fusion.8
  7.7 1.7 fusion.9
  9.4 0.0 all-gather.2.cloned.1.call-update
  9.4 0.0 reduce-scatter.3.cloned.1.call-start
  9.5 0.7 reduce-scatter.3.cloned.1.call-update
  10.2 0.0 reduce-scatter.5.cloned.1.call-start
  10.9 0.1 fusion.5
  11.0 0.7 fusion.19
  11.8 93.6 %all-gather.2.cloned.1.call-done = bf16[384,4096]{1,0:T(8,128)(2,1)} async-done(((bf16[24,4096]{1,0:T(8,128)(2,1)}), bf16[384,4096]{1,0:T(8,128)(2,1)}) %all-gather.2.cloned.1.call-update) | async-done | bytes 3145744 | tf_op jit(solution)/shard_map/all_gather | solution.py:51
  105.4 0.0 copy-done
  105.4 0.0 copy-start.1
  105.4 3.1 convolution_convert_fusion.1
  108.5 0.0 copy-start.4
  108.5 0.1 collective-permute-start.1
  108.6 0.0 copy-done.1
  108.6 4.0 %fusion.43 = f32[384,512]{1,0:T(8,128)S(1)} fusion(bf16[384,4096]{1,0:T(8,128)(2,1)S(1)} %copy-done.1, bf16[4096,512]{1,0:T(8,128)(2,1)} %param.9), kind=kOutput, calls=%fused_computation.55 | convolution fusion | flops 1610612736 | bytes 8126464 | tf_op jit(solution)/shard_map/dot_general | solution.py:54
  112.6 0.3 reshape.175
  112.9 0.0 copy-done.4
  112.9 3.0 convolution_convert_fusion.2
  115.9 2.1 collective-permute-start
  118.0 0.5 fusion.39
  118.4 0.2 subtract_convert_fusion
  118.6 0.0 collective-permute-done.1
  118.7 0.5 subtract_convert_fusion.1
  119.1 2.5 fusion.40
  121.6 0.3 collective-permute-done
  121.9 0.0 copy-start.2
  121.9 2.2 convolution_convert_fusion
  124.1 0.7 copy-done.2
  124.8 4.5 %fusion.44 = f32[384,4096]{1,0:T(8,128)} fusion(bf16[384,512]{0,1:T(8,128)(2,1)S(1)} %bitcast.38, bf16[512,4096]{1,0:T(8,128)(2,1)S(1)} %copy-done.2), kind=kOutput, calls=%fused_computation.56 | convolution fusion | flops 1610612736 | bytes 10878976 | tf_op jit(solution)/shard_map/dot_general | solution.py:93
  129.3 0.0 copy-start.3
  129.3 0.0 reduce-scatter.5.cloned.1.call-update
  129.4 72.2 %reduce-scatter.3.cloned.1.call-done = bf16[24,4096]{1,0:T(8,128)(2,1)} async-done(((bf16[384,4096]{1,0:T(8,128)(2,1)}), bf16[24,4096]{1,0:T(8,128)(2,1)}) %reduce-scatter.3.cloned.1.call-update) | async-done | bytes 196624 | tf_op jit(solution)/shard_map/reduce_scatter | solution.py:42
  201.6 142.6 %reduce-scatter.5.cloned.1.call-done = f32[24,4096]{1,0:T(8,128)} async-done(((f32[384,4096]{1,0:T(8,128)}), f32[24,4096]{1,0:T(8,128)}) %reduce-scatter.5.cloned.1.call-update) | async-done | bytes 393232 | tf_op jit(solution)/shard_map/reduce_scatter | solution.py:92
  344.2 0.0 copy-done.3
  344.2 1.8 fusion.7
  (4 shorter events, 0.0 us)
Async XLA Ops:
  6.5 98.8 %copy-start = (bf16[4096,64]{0,1:T(8,128)(2,1)S(1)}, bf16[4096,64]{0,1:T(8,128)(2,1)}, u32[]{:S(2)}) copy-start(bf16[4096,64]{0,1:T(8,128)(2,1)} %param.10) | copy-start | bytes 1572868
  6.5 98.8 %all-gather.2.cloned.1.call-start = ((), (), s32[]{:S(2)}) async-start(), calls=%async_computation.3 | async-start | bytes 3342336 | tf_op jit(solution)/shard_map/all_gather | solution.py:51
  9.4 192.1 %reduce-scatter.3.cloned.1.call-start = ((), (), s32[]{:S(2)}) async-start(), calls=%async_computation.2 | async-start | bytes 3342336 | tf_op jit(solution)/shard_map/reduce_scatter | solution.py:42
  10.2 334.0 %reduce-scatter.5.cloned.1.call-start = ((), (), s32[]{:S(2)}) async-start(), calls=%async_computation.4 | async-start | bytes 6684672 | tf_op jit(solution)/shard_map/reduce_scatter | solution.py:92
  105.4 3.2 copy-start.1
  108.5 4.4 %copy-start.4 = (bf16[4096,64]{0,1:T(8,128)(2,1)S(1)}, bf16[4096,64]{0,1:T(8,128)(2,1)}, u32[]{:S(2)}) copy-start(bf16[4096,64]{0,1:T(8,128)(2,1)} %param.11) | copy-start | bytes 1572868
  108.5 10.1 %collective-permute-start.1 = (bf16[384,64]{0,1:T(8,128)(2,1)S(1)}, bf16[384,64]{0,1:T(8,128)(2,1)S(1)}, u32[]{:S(2)}, u32[]{:S(2)}) collective-permute-start(bf16[384,64]{0,1:T(8,128)(2,1)S(1)} %convolution_convert_fusion.1), channel_id=1, source_target_pairs={{0,1},{1,0},{2,3},{3,2},{4,5},{5,4},{6,7},{7,6},{8,9},{9,8},{10,11... | collective-permute-start | bytes 147464 | tf_op jit(solution)/shard_map/ppermute | solution.py:11
  115.9 6.0 %collective-permute-start = (bf16[384,64]{0,1:T(8,128)(2,1)S(1)}, bf16[384,64]{0,1:T(8,128)(2,1)S(1)}, u32[]{:S(2)}, u32[]{:S(2)}) collective-permute-start(bf16[384,64]{0,1:T(8,128)(2,1)S(1)} %convolution_convert_fusion.2), channel_id=1, source_target_pairs={{0,1},{1,0},{2,3},{3,2},{4,5},{5,4},{6,7},{7,6},{8,9},{9,8},{10,11... | collective-permute-start | bytes 147464 | tf_op jit(solution)/shard_map/ppermute | solution.py:11
  121.9 2.9 copy-start.2
  129.3 214.8 %copy-start.3 = (bf16[24,4096]{1,0:T(8,128)(2,1)S(1)}, bf16[24,4096]{1,0:T(8,128)(2,1)}, u32[]{:S(2)}) copy-start(bf16[24,4096]{1,0:T(8,128)(2,1)} %param.7) | copy-start | bytes 589828
Sparse Core Ops, SparseCore 0:
  9.5 95.7 all-gather.1
  107.9 93.5 reduce-scatter.2
  204.1 140.0 reduce-scatter.4
where the time goes:
time: 354 us; the launch traced here: 353 us
  waiting for transfers between devices  309 us (87%)
  matrix products  19.3 us (5%)
  between operations  13.9 us (4%)
  other arithmetic  6.19 us (2%)
    reduce_scatter x1, waiting for transfers between devices, per_device(): lax.psum_scatter(jnp.dot(attended, out_weight, preferred_element_type=jnp...  143 us
    all_gather x1, waiting for transfers between devices, per_device(): piece = lax.all_gather(normed_shard, 'tensor', axis=0, tiled=True)  93.6 us
    reduce_scatter x1, waiting for transfers between devices, per_device(): lax.psum_scatter(pending[0].astype(jnp.float32).astype(jnp.bfloat16), 'te...  72.2 us
  transfers between devices with their start and end apart: 5, of which 4 were waited for; matrix products, arithmetic and copies ran while one was open for 6% of the time, Pallas kernels for 0%

commit v1 on v0

v1 whole, which is shorter than its diff:
```python
import functools

import jax
import jax.numpy as jnp
import numpy as np
from jax import lax
from jax.experimental import pallas as pl
from jax.experimental.pallas import tpu as pltpu
from jax.sharding import PartitionSpec as P

MESH = pl.DeviceIdType.MESH
BF16 = jnp.bfloat16
F32 = jnp.float32
rope_base = 500000.0
norm_eps = 1e-05

NX, NZ = 4, 4
D, HD, ROWS = 4096, 128, 384
SHARD = ROWS // (NX * NZ)
BLOCK = SHARD * NZ
HEADS = 4
QW = HEADS * HD
KW = 64
CW = 512
NC = D // CW
ZP, ZM, XP, XM = range(4)


def tables():
    half = HD // 2
    frequency = np.float32(rope_base) ** (
        -np.arange(half, dtype=np.float32) * np.float32(2.0 / HD)
    )
    angles = np.arange(ROWS, dtype=np.float32)[:, None] * frequency[None, :].astype(np.float32)
    cosine, sine = np.cos(angles), np.sin(angles)
    both = np.stack(
        [np.concatenate([cosine, cosine], 1), np.concatenate([-sine, sine], 1)]
    ).astype(np.float32)
    return both.reshape(2, NX, BLOCK, HD)


def kernel(
    plen_ref, res_hbm, pend_hbm, wq_hbm, wk_hbm, wv_hbm, wo_hbm, rope_hbm, out_ref,
    res_v, pend_v, wq_v, wk_v, wv_v, wkv_v, wo_v, rope_v,
    xg, xblk, q_v, kvo, kvr, k_v, v_v, att, fs, fr, ns, nr, racc, zs, zr,
    local_sem, ag_send, ag_recv, kv_send, kv_recv, f_send, f_recv, n_send, n_recv, z_send, z_recv,
):
    t = lax.axis_index("tensor")
    x, z = t // NZ, t % NZ
    xp, xm, xf = (x + 1) % NX, (x + 3) % NX, (x + 2) % NX

    def at(xx, zz):
        return {"tensor": xx * NZ + zz}

    barrier = pltpu.get_barrier_semaphore()
    partners = [at(xp, z), at(xm, z)] + [at(x, (z + j) % NZ) for j in range(1, NZ)]
    for device in partners:
        pl.semaphore_signal(barrier, inc=1, device_id=device, device_id_type=MESH)

    loads = [
        pltpu.make_async_copy(src, dst, local_sem.at[i])
        for i, (src, dst) in enumerate(
            [
                (res_hbm, res_v),
                (wk_hbm, wk_v),
                (wv_hbm, wv_v),
                (wq_hbm, wq_v),
                (rope_hbm, rope_v),
                (wo_hbm, wo_v),
                (pend_hbm, pend_v),
            ]
        )
    ]
    for load in loads:
        load.start()

    loads[0].wait()
    residual = res_v[...].astype(F32)
    scale = lax.rsqrt(jnp.mean(residual * residual, axis=-1, keepdims=True) + norm_eps)
    xg[x, z] = (residual * scale).astype(BF16)

    pl.semaphore_wait(barrier, len(partners))

    def neighbour(way):
        return {
            ZP: at(x, jnp.minimum(z + 1, NZ - 1)),
            ZM: at(x, jnp.maximum(z - 1, 0)),
            XP: at(xp, z),
            XM: at(xm, z),
        }[way]

    def shard_copy(way, xs, zz):
        slot = xs * NZ + zz
        return pltpu.make_async_remote_copy(
            src_ref=xg.at[xs, zz],
            dst_ref=xg.at[xs, zz],
            send_sem=ag_send.at[way, slot],
            recv_sem=ag_recv.at[slot],
            device_id=neighbour(way),
            device_id_type=MESH,
        )

    def level(k, body):
        if k == 0:
            body(z, 0)
        else:
            pl.when(z - k >= 0)(lambda: body(z - k, -1))
            pl.when(z + k < NZ)(lambda: body(z + k, 1))

    def spread(zz, side):
        if side != 0:
            shard_copy(XP, x, zz).wait_recv()
        if side <= 0:
            pl.when(z < NZ - 1)(lambda: shard_copy(ZP, x, zz).start())
        if side >= 0:
            pl.when(z > 0)(lambda: shard_copy(ZM, x, zz).start())
        shard_copy(XP, x, zz).start()
        shard_copy(XM, x, zz).start()

    def pass_on(zz, side):
        shard_copy(XP, xm, zz).wait_recv()
        pl.when(zz % 2 == 0)(lambda: shard_copy(XP, xm, zz).start())
        shard_copy(XM, xp, zz).wait_recv()
        pl.when(zz % 2 == 1)(lambda: shard_copy(XM, xp, zz).start())

    def rotate(value, b):
        return value * rope_v[0, b] + pltpu.roll(value, HD // 2, 1) * rope_v[1, b]

    def kv_copy(b):
        return pltpu.make_async_remote_copy(
            src_ref=kvo.at[b],
            dst_ref=kvr.at[b],
            send_sem=kv_send.at[b],
            recv_sem=kv_recv.at[b],
            device_id=at(x, z + 1 - 2 * (z % 2)),
            device_id_type=MESH,
        )

    def project(b):
        xblk[...] = xg[b].astype(F32).reshape(BLOCK, D).astype(BF16)
        kvo[b] = jnp.dot(xblk[...], wkv_v[...], preferred_element_type=F32).astype(BF16)
        kv_copy(b).start()
        for h in range(0, HEADS, 2):
            pair = jnp.dot(
                xblk[...], wq_v[:, h * HD : (h + 2) * HD], preferred_element_type=F32
            )
            q_v[b, h] = rotate(pair[:, :HD], b).astype(BF16)
            q_v[b, h + 1] = rotate(pair[:, HD:], b).astype(BF16)

    lane = lax.broadcasted_iota(jnp.int32, (BLOCK, HD), 1)
    first_half = lane < KW

    def join(b):
        kv_copy(b).wait_recv()
        own, other = kvo[b].astype(F32), kvr[b].astype(F32)
        even = z % 2 == 0
        low, high = jnp.where(even, own, other), jnp.where(even, other, own)
        key_raw = jnp.where(first_half, low, pltpu.roll(high, KW, 1))
        k_v[b] = rotate(key_raw, b).astype(BF16)
        v_v[b] = jnp.where(first_half, pltpu.roll(low, KW, 1), high).astype(BF16)

    level(0, spread)
    loads[1].wait()
    loads[2].wait()
    wkv_v[...] = jnp.concatenate([wk_v[...], wv_v[...]], axis=1)
    level(1, spread)
    level(0, pass_on)
    level(2, spread)
    level(1, pass_on)
    level(3, spread)
    level(2, pass_on)
    loads[3].wait()
    loads[4].wait()
    project(x)
    level(3, pass_on)
    project(xm)
    project(xp)
    join(x)
    for zz in range(NZ):
        shard_copy(XP, xf, zz).wait_recv()
    project(xf)
    join(xm)
    join(xp)
    join(xf)

    plen = plen_ref[0]

    def attend(b):
        queries = q_v[b].reshape(HEADS * BLOCK, HD)
        keys = k_v[...].reshape(ROWS, HD)
        scores = lax.dot_general(
            queries, keys, (((1,), (1,)), ((), ())), preferred_element_type=F32
        ) * (HD**-0.5)
        row = b * BLOCK + lax.broadcasted_iota(jnp.int32, (BLOCK, ROWS), 0)
        col = lax.broadcasted_iota(jnp.int32, (BLOCK, ROWS), 1)
        allowed = (col <= row) & (col < plen)
        scores = jnp.where(allowed[None], scores.reshape(HEADS, BLOCK, ROWS), -1e30)
        expo = jnp.exp(scores - jnp.max(scores, axis=-1, keepdims=True))
        soft = expo * (1.0 / jnp.sum(expo, axis=-1, keepdims=True))
        result = jnp.dot(
            soft.astype(BF16).reshape(HEADS * BLOCK, ROWS),
            v_v[...].reshape(ROWS, HD),
            preferred_element_type=F32,
        )
        for h in range(HEADS):
            att[b, :, h * HD : (h + 1) * HD] = result[h * BLOCK : (h + 1) * BLOCK].astype(BF16)

    def columns(c):
        return pl.ds(pl.multiple_of(c * CW, CW), CW)

    def partial(b, c):
        return pend_v[b, :, columns(c)].astype(F32) + jnp.dot(
            att[b], wo_v[:, columns(c)], preferred_element_type=F32
        )

    def far_copy(c, way):
        return pltpu.make_async_remote_copy(
            src_ref=fs.at[c], dst_ref=fr.at[c], send_sem=f_send.at[c], recv_sem=f_recv.at[c],
            device_id=neighbour(way), device_id_type=MESH,
        )

    def near_copy(c, way):
        side = 0 if way == XP else 1
        return pltpu.make_async_remote_copy(
            src_ref=ns.at[side, c], dst_ref=nr.at[side, c],
            send_sem=n_send.at[side, c], recv_sem=n_recv.at[side, c],
            device_id=neighbour(way), device_id_type=MESH,
        )

    def z_copy(c, j):
        target = (z + j) % NZ
        return pltpu.make_async_remote_copy(
            src_ref=zs.at[c, target], dst_ref=zr.at[c, j],
            send_sem=z_send.at[c, j], recv_sem=z_recv.at[c, j],
            device_id=at(x, target), device_id_type=MESH,
        )

    attend(xf)
    loads[5].wait()
    loads[6].wait()

    @pl.loop(0, NC // 2)
    def _(i):
        for odd, way in ((0, XP), (1, XM)):
            c = 2 * i + odd
            fs[c] = partial(xf, c).astype(BF16)
            far_copy(c, way).start()

    attend(xp)
    attend(xm)

    @pl.loop(0, NC // 2)
    def _(i):
        for odd, merged, plain in ((0, XP, XM), (1, XM, XP)):
            c = 2 * i + odd
            block_of = {XP: xp, XM: xm}
            side_of = {XP: 0, XM: 1}
            ns[side_of[plain], c] = partial(block_of[plain], c).astype(BF16)
            near_copy(c, plain).start()
            total = partial(block_of[merged], c)
            far_copy(c, merged).wait_recv()
            ns[side_of[merged], c] = (total + fr[c].astype(F32)).astype(BF16)
            near_copy(c, merged).start()

    attend(x)

    @pl.loop(0, NC)
    def _(c):
        total = partial(x, c)
        near_copy(c, XP).wait_recv()
        near_copy(c, XM).wait_recv()
        total = total + nr[0, c].astype(F32) + nr[1, c].astype(F32)
        pieces = total.reshape(NZ, SHARD, CW)
        racc[c] = pieces
        zs[c] = pieces.astype(BF16)
        for j in range(1, NZ):
            z_copy(c, j).start()

    @pl.loop(0, NC)
    def _(c):
        total = res_v[:, columns(c)].astype(F32) + racc[c, z]
        for j in range(1, NZ):
            z_copy(c, j).wait_recv()
            total = total + zr[c, j].astype(F32)
        out_ref[:, columns(c)] = total.astype(BF16)

    for k in range(NZ):
        def sent(zz, side):
            if side <= 0:
                pl.when(z < NZ - 1)(lambda: shard_copy(ZP, x, zz).wait_send())
            if side >= 0:
                pl.when(z > 0)(lambda: shard_copy(ZM, x, zz).wait_send())
            shard_copy(XP, x, zz).wait_send()
            shard_copy(XM, x, zz).wait_send()
            pl.when(zz % 2 == 0)(lambda: shard_copy(XP, xm, zz).wait_send())
            pl.when(zz % 2 == 1)(lambda: shard_copy(XM, xp, zz).wait_send())

        level(k, sent)
    for b in range(NX):
        kv_copy(b).wait_send()

    @pl.loop(0, NC)
    def _(c):
        far_copy(c, XP).wait_send()
        near_copy(c, XP).wait_send()
        near_copy(c, XM).wait_send()
        for j in range(1, NZ):
            z_copy(c, j).wait_send()


def per_device(
    residual_rows, pending, query_weight, key_weight, value_weight, out_weight, prompt_length
):
    hbm = pl.BlockSpec(memory_space=pl.ANY)
    dma = pltpu.SemaphoreType.DMA
    return pl.pallas_call(
        kernel,
        out_shape=jax.ShapeDtypeStruct((SHARD, D), BF16),
        in_specs=[pl.BlockSpec(memory_space=pltpu.SMEM)] + [hbm] * 7,
        out_specs=pl.BlockSpec(memory_space=pltpu.VMEM),
        scratch_shapes=[
            pltpu.VMEM((SHARD, D), BF16),
            pltpu.VMEM((NX, BLOCK, D), BF16),
            pltpu.VMEM((D, QW), BF16),
            pltpu.VMEM((D, KW), BF16),
            pltpu.VMEM((D, KW), BF16),
            pltpu.VMEM((D, 2 * KW), BF16),
            pltpu.VMEM((QW, D), BF16),
            pltpu.VMEM((2, NX, BLOCK, HD), F32),
            pltpu.VMEM((NX, NZ, SHARD, D), BF16),
            pltpu.VMEM((BLOCK, D), BF16),
            pltpu.VMEM((NX, HEADS, BLOCK, HD), BF16),
            pltpu.VMEM((NX, BLOCK, HD), BF16),
            pltpu.VMEM((NX, BLOCK, HD), BF16),
            pltpu.VMEM((NX, BLOCK, HD), BF16),
            pltpu.VMEM((NX, BLOCK, HD), BF16),
            pltpu.VMEM((NX, BLOCK, QW), BF16),
            pltpu.VMEM((NC, BLOCK, CW), BF16),
            pltpu.VMEM((NC, BLOCK, CW), BF16),
            pltpu.VMEM((2, NC, BLOCK, CW), BF16),
            pltpu.VMEM((2, NC, BLOCK, CW), BF16),
            pltpu.VMEM((NC, NZ, SHARD, CW), F32),
            pltpu.VMEM((NC, NZ, SHARD, CW), BF16),
            pltpu.VMEM((NC, NZ, SHARD, CW), BF16),
            dma((7,)),
            dma((4, NX * NZ)),
            dma((NX * NZ,)),
            dma((NX,)),
            dma((NX,)),
            dma((NC,)),
            dma((NC,)),
            dma((2, NC)),
            dma((2, NC)),
            dma((NC, NZ)),
            dma((NC, NZ)),
        ],
        compiler_params=pltpu.CompilerParams(
            collective_id=0, has_side_effects=True, vmem_limit_bytes=48 << 20
        ),
        name="block",
    )(
        prompt_length,
        residual_rows,
        pending.reshape(NX, BLOCK, D),
        query_weight,
        key_weight,
        value_weight,
        out_weight,
        jnp.asarray(tables()),
    )


def solution(mesh):
    placed = (
        P(("dp", "tensor"), None),
        P("tensor", "dp", None),
        P(None, "tensor"),
        P(None, "tensor"),
        P(None, "tensor"),
        P("tensor", None),
        P("dp"),
    )
    return jax.shard_map(
        per_device, mesh=mesh, in_specs=placed, out_specs=P(("dp", "tensor"), None), check_vma=False
    )
```

time: 354 us -> 77.9 us (0.22)
  waiting for transfers between devices: 309 us -> 0 us
  Pallas kernels: 0 us -> 69.4 us
  matrix products: 19.3 us -> 0 us
  between operations: 13.9 us -> 0.68 us
  other arithmetic: 6.19 us -> 0 us
  local copies, waits for them, and re-layouts: 1.46 us -> 7.52 us
    reduce_scatter x2 -> x0, waiting for transfers between devices: 215 us -> none  [the longest x1 143 us: per_device(): lax.psum_scatter(jnp.dot(attended, out_weight, preferred_element_type=jnp...]
    all_gather x1 -> x0, waiting for transfers between devices: 93.6 us -> none  [per_device(): piece = lax.all_gather(normed_shard, 'tensor', axis=0, tiled=True)]
    pallas_call x0 -> x1, Pallas kernels: none -> 69.4 us  [per_device(): pl.pallas_call(kernel, out_shape=jax.ShapeDtypeStruct((SHARD, D), BF16),...]
    dot_general x5 -> x0, matrix products: 16.9 us -> none  [the longest x1 4.54 us: per_device(): jnp.dot(attended, out_weight, preferred_element_type=jnp.float32)]
    unnamed x10 -> x9, local copies, waits for them, and re-layouts: 0.72 us -> 7.52 us
  transfers between devices with their start and end apart: 5 -> 0, of which waited for: 4 -> 0; matrix products, arithmetic and copies ran while one was open for 6% -> 0% of each run, Pallas kernels for 0% -> 0%
where the time goes in v1:
time: 77.9 us; the launch traced here: 77.6 us
  Pallas kernels  69.4 us (89%)
  local copies, waits for them, and re-layouts  7.52 us (10%)
    pallas_call x1, Pallas kernels, per_device(): pl.pallas_call(kernel, out_shape=jax.ShapeDtypeStruct((SHARD, D), BF16),...  69.4 us
    unnamed x9, local copies, waits for them, and re-layouts  7.52 us

profile of v1, /device:TPU:16, one launch (start us, length us, event | category | flops | bytes accessed | tf_op | source)
XLA Modules:
  0.0 77.6 jit_solution(17728848732945093146)
XLA Ops:
  0.7 1.5 %copy.9.wk_hbm = bf16[4096,64]{1,0:T(8,128)(2,1)S(1)} copy(bf16[4096,64]{0,1:T(8,128)(2,1)} %param.11) | data formatting | bytes 1048576 | tf_op args[3]
  2.2 1.5 %copy.10.wv_hbm = bf16[4096,64]{1,0:T(8,128)(2,1)S(1)} copy(bf16[4096,64]{0,1:T(8,128)(2,1)} %param.12) | data formatting | bytes 1048576 | tf_op args[4]
  3.7 0.0 copy-start
  3.7 1.9 %copy-done = bf16[1,384,4096]{2,1,0:T(8,128)(2,1)S(1)} copy-done((bf16[1,384,4096]{2,1,0:T(8,128)(2,1)S(1)}, bf16[1,384,4096]{2,1,0:T(8,128)(2,1)}, u32[]{:S(2)}) %copy-start) | copy-done | bytes 3145752
  5.6 0.0 copy-start.1
  5.6 1.0 %copy-done.1 = f32[2,4,96,128]{3,2,1,0:T(8,128)S(1)} copy-done((f32[2,4,96,128]{3,2,1,0:T(8,128)S(1)}, f32[2,4,96,128]{3,2,1,0:T(8,128)}, u32[]{:S(2)}) %copy-start.1) | copy-done | bytes 393240
  6.6 0.0 copy-start.2
  6.6 0.9 %copy-done.2 = bf16[24,4096]{1,0:T(8,128)(2,1)S(1)} copy-done((bf16[24,4096]{1,0:T(8,128)(2,1)S(1)}, bf16[24,4096]{1,0:T(8,128)(2,1)}, u32[]{:S(2)}) %copy-start.2) | copy-done | bytes 196632
  7.5 69.4 %block.1 = bf16[24,4096]{1,0:T(8,128)(2,1)S(1)} custom-call(s32[1]{0:T(128)S(6)} %copy.12.plen_ref, bf16[24,4096]{1,0:T(8,128)(2,1)S(1)} %copy-done.2, bf16[4,96,4096]{2,1,0:T(8,128)(2,1)S(1)} %bitcast.1, bf16[4096,512]{1,0:T(8,128)(2,1)} %wq_hbm.1, bf16[4096,64]{1,0:T(8,128)(2,1)S(1)} %copy.9.wk_hbm, bf16[4096,64]{1,0:T(8,128)(2,1)S(1)} %copy.10.wv_hbm, ...), custom_call_target="tpu_custom_call" | custom-call | tf_op jit(solution)/shard_map/block/pallas_call | solution.py:316
  76.9 0.7 copy.13
Async XLA Ops:
  3.7 1.9 %copy-start = (bf16[1,384,4096]{2,1,0:T(8,128)(2,1)S(1)}, bf16[1,384,4096]{2,1,0:T(8,128)(2,1)}, u32[]{:S(2)}) copy-start(bf16[1,384,4096]{2,1,0:T(8,128)(2,1)} %param.9) | copy-start | bytes 9437188
  5.6 1.0 %copy-start.1 = (f32[2,4,96,128]{3,2,1,0:T(8,128)S(1)}, f32[2,4,96,128]{3,2,1,0:T(8,128)}, u32[]{:S(2)}) copy-start(f32[2,4,96,128]{3,2,1,0:T(8,128)} %constant.2.clone.rope_hbm) | copy-start | bytes 1179652
  6.6 0.9 %copy-start.2 = (bf16[24,4096]{1,0:T(8,128)(2,1)S(1)}, bf16[24,4096]{1,0:T(8,128)(2,1)}, u32[]{:S(2)}) copy-start(bf16[24,4096]{1,0:T(8,128)(2,1)} %res_hbm.1) | copy-start | bytes 589828

commit v2 on v1

v2 whole, which is shorter than its diff:
```python
import functools

import jax
import jax.numpy as jnp
import numpy as np
from jax import lax
from jax.experimental import pallas as pl
from jax.experimental.pallas import tpu as pltpu
from jax.sharding import PartitionSpec as P

MESH = pl.DeviceIdType.MESH
BF16 = jnp.bfloat16
F32 = jnp.float32
rope_base = 500000.0
norm_eps = 1e-05

NX, NZ = 4, 4
D, HD, ROWS = 4096, 128, 384
SHARD = ROWS // (NX * NZ)
BLOCK = SHARD * NZ
HEADS = 4
QW = HEADS * HD
KW = 64
ZP, ZM, XP, XM = range(4)
Z_ORDER = (1, 3, 2)
GB, GP = 512, 2
GW = (D - GB) // GP
SB, CW, PAIRS, AHEAD, BEHIND = 512, 256, 7, 3, 2
NC, PW = 2 * PAIRS, 2 * CW
B1, B2 = PAIRS - 1, PAIRS
FAR, PLUS, MINUS, OWN = range(4)


def tables():
    half = HD // 2
    frequency = np.float32(rope_base) ** (
        -np.arange(half, dtype=np.float32) * np.float32(2.0 / HD)
    )
    angles = np.arange(ROWS, dtype=np.float32)[:, None] * frequency[None, :].astype(np.float32)
    cosine, sine = np.cos(angles), np.sin(angles)
    both = np.stack(
        [np.concatenate([cosine, cosine], 1), np.concatenate([-sine, sine], 1)]
    ).astype(np.float32)
    return both.reshape(2, NX, BLOCK, HD)


def kernel(
    plen_ref, res_hbm, pend_hbm, wq_hbm, wk_hbm, wv_hbm, wo_hbm, rope_hbm, out_ref,
    res_v, pend_v, wq_v, wkv_v, wo_v, rope_v,
    xg, acc, q_v, kvo, kvr, k_v, v_v, att, fs, fr, ns, nr, own, zs, zr,
    pb, bzs, bzr, bsum, bfs, bfr, bns, bnr,
    local_sem, az_send, az_recv, ax_send, ax_recv, ab_send, ab_recv, kv_send, kv_recv,
    f_send, f_recv, n_send, n_recv, z_send, z_recv,
    bz_send, bz_recv, bf_send, bf_recv, bn_send, bn_recv,
):
    t = lax.axis_index("tensor")
    x, z = t // NZ, t % NZ
    xp, xm, xf = (x + 1) % NX, (x + 3) % NX, (x + 2) % NX

    def at(xx, zz):
        return {"tensor": xx * NZ + zz}

    barrier = pltpu.get_barrier_semaphore()
    partners = [at(xp, z), at(xm, z)] + [at(x, (z + j) % NZ) for j in range(1, NZ)]
    for device in partners:
        pl.semaphore_signal(barrier, inc=1, device_id=device, device_id_type=MESH)

    loads = [
        pltpu.make_async_copy(src, dst, local_sem.at[i])
        for i, (src, dst) in enumerate(
            [
                (res_hbm, res_v),
                (wk_hbm, wkv_v.at[:KW]),
                (wv_hbm, wkv_v.at[KW:]),
                (wq_hbm, wq_v),
                (rope_hbm, rope_v),
                (wo_hbm, wo_v),
                (pend_hbm, pend_v),
            ]
        )
    ]
    for load in loads:
        load.start()

    loads[0].wait()
    residual = res_v[...].astype(F32)
    scale = lax.rsqrt(jnp.mean(residual * residual, axis=-1, keepdims=True) + norm_eps)
    xg[x, z] = (residual * scale).astype(BF16)

    pl.semaphore_wait(barrier, len(partners))

    def neighbour(way):
        return {
            ZP: at(x, jnp.minimum(z + 1, NZ - 1)),
            ZM: at(x, jnp.maximum(z - 1, 0)),
            XP: at(xp, z),
            XM: at(xm, z),
        }[way]

    def remote(src, dst, send, recv, device):
        return pltpu.make_async_remote_copy(
            src_ref=src, dst_ref=dst, send_sem=send, recv_sem=recv,
            device_id=device, device_id_type=MESH,
        )

    def cols_a(p):
        return pl.ds(GB + p * GW, GW)

    def az_copy(way, zz, p):
        ref = xg.at[x, zz, :, cols_a(p)]
        return remote(ref, ref, az_send.at[way, zz, p], az_recv.at[zz, p], neighbour(way))

    def ax_copy(way, xs, zz, p):
        ref = xg.at[xs, zz, :, cols_a(p)]
        return remote(
            ref, ref, ax_send.at[way - XP, xs, zz, p], ax_recv.at[xs, zz, p], neighbour(way)
        )

    def bx_copy(way, xs, part):
        lo, width = ((0, GB), (0, GB // 2), (GB // 2, GB // 2))[part]
        ref = xg.at[xs, z, :, pl.ds(lo, width)]
        return remote(
            ref, ref, ab_send.at[way - XP, xs, part], ab_recv.at[xs, z, part], neighbour(way)
        )

    def bz_copy(xs, j, source=0):
        zz = (z + source) % NZ
        ref = xg.at[xs, zz, :, pl.ds(0, GB)]
        return remote(
            ref, ref, ab_send.at[1 + j, xs, 3], ab_recv.at[xs, zz, 0], at(x, (z + j) % NZ)
        )

    sends = []

    def started(copy, when=None, only_note=False):
        if not only_note:
            copy.start() if when is None else pl.when(when)(copy.start)
        sends.append((copy, when))

    def level(k, body):
        if k == 0:
            body(z, 0, None)
        else:
            body(jnp.maximum(z - k, 0), -1, z - k >= 0)
            body(jnp.minimum(z + k, NZ - 1), 1, z + k < NZ)

    def spread(p, zz, side, when):
        way, more = (ZP, z < NZ - 1) if side < 0 else (ZM, z > 0)

        @pl.when(when)
        def _():
            az_copy(way, zz, p).wait_recv()
            pl.when(more)(lambda: az_copy(way, zz, p).start())
            ax_copy(XP, x, zz, p).start()
            ax_copy(XM, x, zz, p).start()

        started(az_copy(way, zz, p), when & more, only_note=True)
        started(ax_copy(XP, x, zz, p), when, only_note=True)
        started(ax_copy(XM, x, zz, p), when, only_note=True)

    def pass_on(p, zz, side, when):
        onward = ax_copy(XP, xm, zz, p) if p % 2 == 0 else ax_copy(XM, xp, zz, p)

        def body():
            ax_copy(XP, xm, zz, p).wait_recv()
            if p % 2 == 0:
                onward.start()
            ax_copy(XM, xp, zz, p).wait_recv()
            if p % 2 == 1:
                onward.start()

        body() if when is None else pl.when(when)(body)
        started(onward, when, only_note=True)

    def each(body, k):
        for p in range(GP):
            level(k, functools.partial(body, p))

    def rotate(value, b):
        return value * rope_v[0, b] + pltpu.roll(value, HD // 2, 1) * rope_v[1, b]

    def kv_copy(b):
        return remote(
            kvo.at[b], kvr.at[b], kv_send.at[b], kv_recv.at[b], at(x, z + 1 - 2 * (z % 2))
        )

    def project(b, lo, width, first=False):
        rows = xg[b, :, :, lo : lo + width].reshape(BLOCK, width)
        queries = jnp.dot(rows, wq_v[lo : lo + width], preferred_element_type=F32)
        others = lax.dot_general(
            rows, wkv_v[:, lo : lo + width], (((1,), (1,)), ((), ())), preferred_element_type=F32
        )
        if first:
            acc[b, :, :QW] = queries
            acc[b, :, QW:] = others
        else:
            acc[b, :, :QW] += queries
            acc[b, :, QW:] += others

    def finish(b):
        kvo[b] = acc[b, :, QW:].astype(BF16)
        kv_copy(b).start()
        for h in range(HEADS):
            q_v[b, h] = rotate(acc[b, :, h * HD : (h + 1) * HD], b).astype(BF16)

    first_half = lax.broadcasted_iota(jnp.int32, (BLOCK, HD), 1) < KW

    def join(b):
        kv_copy(b).wait_recv()
        own, other = kvo[b].astype(F32), kvr[b].astype(F32)
        even = z % 2 == 0
        low, high = jnp.where(even, own, other), jnp.where(even, other, own)
        key_raw = jnp.where(first_half, low, pltpu.roll(high, KW, 1))
        k_v[b] = rotate(key_raw, b).astype(BF16)
        v_v[b] = jnp.where(first_half, pltpu.roll(low, KW, 1), high).astype(BF16)

    started(bx_copy(XP, x, 0))
    started(bx_copy(XM, x, 0))
    for p in range(GP):
        started(az_copy(ZP, z, p), z < NZ - 1)
        started(az_copy(ZM, z, p), z > 0)
        started(ax_copy(XP, x, z, p))
        started(ax_copy(XM, x, z, p))
    each(spread, 1)
    each(pass_on, 0)
    each(spread, 2)
    for j in Z_ORDER:
        started(bz_copy(x, j))
    bx_copy(XP, xm, 0).wait_recv()
    started(bx_copy(XP, xm, 1))
    bx_copy(XM, xp, 0).wait_recv()
    started(bx_copy(XM, xp, 2))
    for xs in (xm, xp):
        for j in Z_ORDER:
            started(bz_copy(xs, j))
    each(pass_on, 1)
    each(spread, 3)
    bx_copy(XP, xf, 1).wait_recv()
    bx_copy(XP, xf, 2).wait_recv()
    for j in Z_ORDER:
        started(bz_copy(xf, j))
    each(pass_on, 2)
    for load in loads[1:5]:
        load.wait()
    project(x, GB, D - GB, first=True)
    each(pass_on, 3)
    project(xm, GB, D - GB, first=True)
    project(xp, GB, D - GB, first=True)
    for xs in (x, xm, xp, xf):
        for j in range(1, NZ):
            bz_copy(xs, 1, source=j).wait_recv()
        project(xs, 0, GB, first=xs is xf)
        if xs is not xf:
            finish(xs)
    for p in range(0, GP, 2):
        for pp in (p, p + 1):
            for zz in range(NZ):
                ax_copy(XP, xf, zz, pp).wait_recv()
        project(xf, GB + p * GW, 2 * GW)
    finish(xf)
    for xs in (x, xm, xp, xf):
        join(xs)

    plen = plen_ref[0]

    def attend(place):
        b = (xf, xp, xm, x)[place]
        queries = q_v[b].reshape(HEADS * BLOCK, HD)
        keys = k_v[...].reshape(ROWS, HD)
        scores = lax.dot_general(
            queries, keys, (((1,), (1,)), ((), ())), preferred_element_type=F32
        ) * (HD**-0.5)
        row = b * BLOCK + lax.broadcasted_iota(jnp.int32, (BLOCK, ROWS), 0)
        col = lax.broadcasted_iota(jnp.int32, (BLOCK, ROWS), 1)
        allowed = (col <= row) & (col < plen)
        scores = jnp.where(allowed[None], scores.reshape(HEADS, BLOCK, ROWS), -1e30)
        expo = jnp.exp(scores - jnp.max(scores, axis=-1, keepdims=True))
        soft = expo * (1.0 / jnp.sum(expo, axis=-1, keepdims=True))
        result = jnp.dot(
            soft.astype(BF16).reshape(HEADS * BLOCK, ROWS),
            v_v[...].reshape(ROWS, HD),
            preferred_element_type=F32,
        )
        for h in range(HEADS):
            att[place, :, h * HD : (h + 1) * HD] = result[h * BLOCK : (h + 1) * BLOCK].astype(BF16)

    def columns(i):
        return pl.ds(pl.multiple_of(SB + i * PW, HD), PW)

    def partial(places, cols):
        rows = att[places.start : places.stop].reshape(len(places) * BLOCK, QW)
        product = jnp.dot(rows, wo_v[:, cols], preferred_element_type=F32)
        return [
            pend_v[(xf, xp, xm, x)[place], :, cols].astype(F32)
            + product[k * BLOCK : (k + 1) * BLOCK]
            for k, place in enumerate(places)
        ]

    side = {XP: 0, XM: 1}

    def f_copy(c, way):
        return remote(fs.at[c], fr.at[c], f_send.at[0], f_recv.at[c], neighbour(way))

    def n_copy(c, way):
        s = side[way]
        return remote(ns.at[s, c], nr.at[s, c], n_send.at[0], n_recv.at[s, c], neighbour(way))

    def z_copy(i, j):
        target = (z + j) % NZ
        return remote(zs.at[i, target], zr.at[i, j], z_send.at[0], z_recv.at[i, j], at(x, target))

    def rz_copy(j):
        target = (z + j) % NZ
        return remote(bzs.at[target], bzr.at[j], bz_send.at[j], bz_recv.at[j], at(x, target))

    def rf_copy(way):
        s = side[way]
        return remote(bfs.at[s], bfr.at[s], bf_send.at[s], bf_recv.at[s], neighbour(way))

    def rn_copy(way):
        s = side[way]
        return remote(bns.at[s], bnr.at[s], bn_send.at[s], bn_recv.at[s], neighbour(way))

    def send_far(i):
        (total,) = partial(range(FAR, FAR + 1), columns(i))
        for odd, way in ((0, XP), (1, XM)):
            c = 2 * i + odd
            fs[c] = total[:, odd * CW : (odd + 1) * CW].astype(BF16)
            f_copy(c, way).start()

    def send_near(i):
        plus, minus, mine = partial(range(PLUS, OWN + 1), columns(i))
        c, d = 2 * i, 2 * i + 1
        ns[0, d] = plus[:, CW:].astype(BF16)
        n_copy(d, XP).start()
        ns[1, c] = minus[:, :CW].astype(BF16)
        n_copy(c, XM).start()
        own[i] = mine
        f_copy(c, XP).wait_recv()
        ns[0, c] = (plus[:, :CW] + fr[c].astype(F32)).astype(BF16)
        n_copy(c, XP).start()
        f_copy(d, XM).wait_recv()
        ns[1, d] = (minus[:, CW:] + fr[d].astype(F32)).astype(BF16)
        n_copy(d, XM).start()

    def send_z(i):
        for odd in (0, 1):
            c, cols = 2 * i + odd, slice(odd * CW, (odd + 1) * CW)
            n_copy(c, XP).wait_recv()
            n_copy(c, XM).wait_recv()
            total = own[i, :, cols] + nr[0, c].astype(F32) + nr[1, c].astype(F32)
            own[i, :, cols] = total
            zs[i, :, :, cols] = total.reshape(NZ, SHARD, CW).astype(BF16)
        for j in Z_ORDER:
            z_copy(i, j).start()

    attend(FAR)
    loads[5].wait()
    loads[6].wait()
    pl.loop(0, AHEAD)(send_far)
    for place in (PLUS, MINUS, OWN):
        attend(place)
    for place, total in enumerate(partial(range(NX), pl.ds(0, SB))):
        pieces = total.reshape(NZ, SHARD, SB)
        pb[place] = pieces
        bzs[:, place] = pieces.astype(BF16)
    for j in Z_ORDER:
        rz_copy(j).start()

    @pl.loop(0, PAIRS + BEHIND)
    def _(i):
        pl.when(i + AHEAD < PAIRS)(lambda: send_far(i + AHEAD))
        pl.when(i < PAIRS)(lambda: send_near(i))
        pl.when(i >= BEHIND)(lambda: send_z(i - BEHIND))

        @pl.when(i == 1)
        def _():
            for copy, when in sends:
                copy.wait_send() if when is None else pl.when(when)(copy.wait_send)
            for b in range(NX):
                kv_copy(b).wait_send()

        @pl.when(i == B1)
        def _():
            for j in range(1, NZ):
                rz_copy(j).wait_recv()
            for place in range(NX):
                total = pb[place, z]
                for j in range(1, NZ):
                    total = total + bzr[j, place].astype(F32)
                bsum[place] = total
            bfs[0] = bsum[FAR, :, : SB // 2].astype(BF16)
            bfs[1] = bsum[FAR, :, SB // 2 :].astype(BF16)
            rf_copy(XP).start()
            rf_copy(XM).start()

        @pl.when(i == B2)
        def _():
            rf_copy(XP).wait_recv()
            rf_copy(XM).wait_recv()
            bns[0, :, : SB // 2] = (bsum[PLUS, :, : SB // 2] + bfr[0].astype(F32)).astype(BF16)
            bns[0, :, SB // 2 :] = bsum[PLUS, :, SB // 2 :].astype(BF16)
            bns[1, :, : SB // 2] = bsum[MINUS, :, : SB // 2].astype(BF16)
            bns[1, :, SB // 2 :] = (bsum[MINUS, :, SB // 2 :] + bfr[1].astype(F32)).astype(BF16)
            rn_copy(XP).start()
            rn_copy(XM).start()

    remote(fs, fr, f_send.at[0], f_recv.at[0], neighbour(XP)).wait_send()
    remote(ns, nr, n_send.at[0], n_recv.at[0, 0], neighbour(XP)).wait_send()
    for j in range(1, NZ):
        rz_copy(j).wait_send()
    for way in (XP, XM):
        rf_copy(way).wait_send()

    @pl.loop(0, PAIRS)
    def _(i):
        mine = own[i].reshape(NZ, SHARD, PW)
        total = jnp.where(z == 0, mine[0], jnp.where(z == 1, mine[1], jnp.where(z == 2, mine[2], mine[3])))
        total = total + res_v[:, columns(i)].astype(F32)
        for j in range(1, NZ):
            z_copy(i, j).wait_recv()
            total = total + zr[i, j].astype(F32)
        out_ref[:, columns(i)] = total.astype(BF16)

    rn_copy(XP).wait_recv()
    rn_copy(XM).wait_recv()
    out_ref[:, :SB] = (
        res_v[:, :SB].astype(F32) + bsum[OWN] + bnr[0].astype(F32) + bnr[1].astype(F32)
    ).astype(BF16)
    rn_copy(XP).wait_send()
    rn_copy(XM).wait_send()
    sent = zs.at[:, 1:]
    remote(sent, sent, z_send.at[0], z_recv.at[0, 0], neighbour(XP)).wait_send()


def per_device(
    residual_rows, pending, query_weight, key_weight, value_weight, out_weight, prompt_length
):
    hbm = pl.BlockSpec(memory_space=pl.ANY)
    dma = pltpu.SemaphoreType.DMA
    return pl.pallas_call(
        kernel,
        out_shape=jax.ShapeDtypeStruct((SHARD, D), BF16),
        in_specs=[pl.BlockSpec(memory_space=pltpu.SMEM)] + [hbm] * 7,
        out_specs=pl.BlockSpec(memory_space=pltpu.VMEM),
        scratch_shapes=[
            pltpu.VMEM((SHARD, D), BF16),
            pltpu.VMEM((NX, BLOCK, D), BF16),
            pltpu.VMEM((D, QW), BF16),
            pltpu.VMEM((2 * KW, D), BF16),
            pltpu.VMEM((QW, D), BF16),
            pltpu.VMEM((2, NX, BLOCK, HD), F32),
            pltpu.VMEM((NX, NZ, SHARD, D), BF16),
            pltpu.VMEM((NX, BLOCK, QW + 2 * KW), F32),
            pltpu.VMEM((NX, HEADS, BLOCK, HD), BF16),
            pltpu.VMEM((NX, BLOCK, HD), BF16),
            pltpu.VMEM((NX, BLOCK, HD), BF16),
            pltpu.VMEM((NX, BLOCK, HD), BF16),
            pltpu.VMEM((NX, BLOCK, HD), BF16),
            pltpu.VMEM((NX, BLOCK, QW), BF16),
            pltpu.VMEM((NC, BLOCK, CW), BF16),
            pltpu.VMEM((NC, BLOCK, CW), BF16),
            pltpu.VMEM((2, NC, BLOCK, CW), BF16),
            pltpu.VMEM((2, NC, BLOCK, CW), BF16),
            pltpu.VMEM((PAIRS, BLOCK, PW), F32),
            pltpu.VMEM((PAIRS, NZ, SHARD, PW), BF16),
            pltpu.VMEM((PAIRS, NZ, SHARD, PW), BF16),
            pltpu.VMEM((NX, NZ, SHARD, SB), F32),
            pltpu.VMEM((NZ, NX, SHARD, SB), BF16),
            pltpu.VMEM((NZ, NX, SHARD, SB), BF16),
            pltpu.VMEM((NX, SHARD, SB), F32),
            pltpu.VMEM((2, SHARD, SB // 2), BF16),
            pltpu.VMEM((2, SHARD, SB // 2), BF16),
            pltpu.VMEM((2, SHARD, SB), BF16),
            pltpu.VMEM((2, SHARD, SB), BF16),
            dma((7,)),
            dma((2, NZ, GP)),
            dma((NZ, GP)),
            dma((2, NX, NZ, GP)),
            dma((NX, NZ, GP)),
            dma((1 + NZ, NX, 4)),
            dma((NX, NZ, 3)),
            dma((NX,)),
            dma((NX,)),
            dma((1,)),
            dma((NC,)),
            dma((1,)),
            dma((2, NC)),
            dma((1,)),
            dma((PAIRS, NZ)),
            dma((NZ,)),
            dma((NZ,)),
            dma((2,)),
            dma((2,)),
            dma((2,)),
            dma((2,)),
        ],
        compiler_params=pltpu.CompilerParams(
            collective_id=0, has_side_effects=True, vmem_limit_bytes=63 << 20
        ),
        name="block",
    )(
        prompt_length,
        residual_rows,
        pending.reshape(NX, BLOCK, D),
        query_weight,
        key_weight.T,
        value_weight.T,
        out_weight,
        jnp.asarray(tables()),
    )


def solution(mesh):
    placed = (
        P(("dp", "tensor"), None),
        P("tensor", "dp", None),
        P(None, "tensor"),
        P(None, "tensor"),
        P(None, "tensor"),
        P("tensor", None),
        P("dp"),
    )
    return jax.shard_map(
        per_device, mesh=mesh, in_specs=placed, out_specs=P(("dp", "tensor"), None), check_vma=False
    )
```

time: 77.9 us -> 70.5 us (0.905)
  local copies, waits for them, and re-layouts: 7.52 us -> 1.62 us
  Pallas kernels: 69.4 us -> 68.1 us
    unnamed x9 -> x1, local copies, waits for them, and re-layouts: 7.52 us -> 1.62 us
    pallas_call x1, Pallas kernels: 69.4 us -> 68.1 us  [per_device(): pl.pallas_call(kernel, out_shape=jax.ShapeDtypeStruct((SHARD, D), BF16),...]
where the time goes in v2:
time: 70.5 us; the launch traced here: 70.4 us
  Pallas kernels  68.1 us (97%)
  local copies, waits for them, and re-layouts  1.62 us (2%)
    pallas_call x1, Pallas kernels, per_device(): pl.pallas_call(kernel, out_shape=jax.ShapeDtypeStruct((SHARD, D), BF16),...  68.1 us
    unnamed x1, local copies, waits for them, and re-layouts  1.62 us

profile of v2, /device:TPU:16, one launch (start us, length us, event | category | flops | bytes accessed | tf_op | source)
XLA Modules:
  0.0 70.4 jit_solution(4948537114341046161)
XLA Ops:
  0.7 68.1 %block.1 = bf16[24,4096]{1,0:T(8,128)(2,1)} custom-call(s32[1]{0:T(128)S(6)} %copy.10.plen_ref, bf16[24,4096]{1,0:T(8,128)(2,1)} %res_hbm.1, bf16[4,96,4096]{2,1,0:T(8,128)(2,1)} %bitcast.3, bf16[4096,512]{1,0:T(8,128)(2,1)} %wq_hbm.1, bf16[64,4096]{1,0:T(8,128)(2,1)} %bitcast.4, bf16[64,4096]{1,0:T(8,128)(2,1)} %bitcast.5, bf16[512,4096]{1,0:T(8,128)(2,1)} %wo_hbm.1, ...), custom_call_target="tpu_custom_call" | custom-call | tf_op jit(solution)/shard_map/block/pallas_call | solution.py:441
  68.7 1.6 %copy.11 = bf16[24,4096]{1,0:T(8,128)(2,1)} copy(bf16[24,4096]{1,0:T(8,128)(2,1)} %block.1) | data formatting | bytes 393216

commit v3 on v2

--- a/solution.py
+++ b/solution.py
@@ -23,7 +23,7 @@
 KW = 64
 ZP, ZM, XP, XM = range(4)
 Z_ORDER = (1, 3, 2)
-GB, GP = 512, 2
+GB, GP = 768, 2
 GW = (D - GB) // GP
 SB, CW, PAIRS, AHEAD, BEHIND = 512, 256, 7, 3, 2
 NC, PW = 2 * PAIRS, 2 * CW
@@ -46,7 +46,7 @@
 
 def kernel(
     plen_ref, res_hbm, pend_hbm, wq_hbm, wk_hbm, wv_hbm, wo_hbm, rope_hbm, out_ref,
-    res_v, pend_v, wq_v, wkv_v, wo_v, rope_v,
+    res_v, pend_v, w_v, wkv_v, wo_v, rope_v,
     xg, acc, q_v, kvo, kvr, k_v, v_v, att, fs, fr, ns, nr, own, zs, zr,
     pb, bzs, bzr, bsum, bfs, bfr, bns, bnr,
     local_sem, az_send, az_recv, ax_send, ax_recv, ab_send, ab_recv, kv_send, kv_recv,
@@ -72,7 +72,7 @@
                 (res_hbm, res_v),
                 (wk_hbm, wkv_v.at[:KW]),
                 (wv_hbm, wkv_v.at[KW:]),
-                (wq_hbm, wq_v),
+                (wq_hbm, w_v.at[:, :QW]),
                 (rope_hbm, rope_v),
                 (wo_hbm, wo_v),
                 (pend_hbm, pend_v),
@@ -184,22 +184,19 @@
             kvo.at[b], kvr.at[b], kv_send.at[b], kv_recv.at[b], at(x, z + 1 - 2 * (z % 2))
         )
 
-    def project(b, lo, width, first=False):
+    def project(b, lo, width, first=False, part=slice(0, QW + 2 * KW)):
         rows = xg[b, :, :, lo : lo + width].reshape(BLOCK, width)
-        queries = jnp.dot(rows, wq_v[lo : lo + width], preferred_element_type=F32)
-        others = lax.dot_general(
-            rows, wkv_v[:, lo : lo + width], (((1,), (1,)), ((), ())), preferred_element_type=F32
-        )
+        result = jnp.dot(rows, w_v[lo : lo + width, part], preferred_element_type=F32)
         if first:
-            acc[b, :, :QW] = queries
-            acc[b, :, QW:] = others
+            acc[b, :, part] = result
         else:
-            acc[b, :, :QW] += queries
-            acc[b, :, QW:] += others
-
-    def finish(b):
+            acc[b, :, part] += result
+
+    def finish_kv(b):
         kvo[b] = acc[b, :, QW:].astype(BF16)
         kv_copy(b).start()
+
+    def finish_q(b):
         for h in range(HEADS):
             q_v[b, h] = rotate(acc[b, :, h * HD : (h + 1) * HD], b).astype(BF16)
 
@@ -221,6 +218,14 @@
         started(az_copy(ZM, z, p), z > 0)
         started(ax_copy(XP, x, z, p))
         started(ax_copy(XM, x, z, p))
+    for load in loads[1:3]:
+        load.wait()
+
+    @pl.loop(0, D // QW)
+    def _(i):
+        rows = pl.ds(pl.multiple_of(i * QW, QW), QW)
+        w_v[rows, QW:] = wkv_v[:, rows].astype(F32).T.astype(BF16)
+
     each(spread, 1)
     each(pass_on, 0)
     each(spread, 2)
@@ -240,7 +245,7 @@
     for j in Z_ORDER:
         started(bz_copy(xf, j))
     each(pass_on, 2)
-    for load in loads[1:5]:
+    for load in loads[3:5]:
         load.wait()
     project(x, GB, D - GB, first=True)
     each(pass_on, 3)
@@ -251,15 +256,20 @@
             bz_copy(xs, 1, source=j).wait_recv()
         project(xs, 0, GB, first=xs is xf)
         if xs is not xf:
-            finish(xs)
-    for p in range(0, GP, 2):
-        for pp in (p, p + 1):
-            for zz in range(NZ):
-                ax_copy(XP, xf, zz, pp).wait_recv()
-        project(xf, GB + p * GW, 2 * GW)
-    finish(xf)
-    for xs in (x, xm, xp, xf):
+            finish_kv(xs)
+            finish_q(xs)
+    for xs in (x, xm, xp):
         join(xs)
+    for p in range(GP):
+        for zz in range(NZ):
+            ax_copy(XP, xf, zz, p).wait_recv()
+        if p < GP - 1:
+            project(xf, GB + p * GW, GW)
+    project(xf, GB + (GP - 1) * GW, GW, part=slice(QW, QW + 2 * KW))
+    finish_kv(xf)
+    project(xf, GB + (GP - 1) * GW, GW, part=slice(0, QW))
+    finish_q(xf)
+    join(xf)
 
     plen = plen_ref[0]
 
@@ -436,7 +446,7 @@
 def per_device(
     residual_rows, pending, query_weight, key_weight, value_weight, out_weight, prompt_length
 ):
-    hbm = pl.BlockSpec(memory_space=pl.ANY)
+    hbm = pl.BlockSpec(memory_space=pltpu.HBM)
     dma = pltpu.SemaphoreType.DMA
     return pl.pallas_call(
         kernel,
@@ -446,7 +456,7 @@
         scratch_shapes=[
             pltpu.VMEM((SHARD, D), BF16),
             pltpu.VMEM((NX, BLOCK, D), BF16),
-            pltpu.VMEM((D, QW), BF16),
+            pltpu.VMEM((D, QW + 2 * KW), BF16),
             pltpu.VMEM((2 * KW, D), BF16),
             pltpu.VMEM((QW, D), BF16),
             pltpu.VMEM((2, NX, BLOCK, HD), F32),
@@ -496,7 +506,7 @@
             dma((2,)),
         ],
         compiler_params=pltpu.CompilerParams(
-            collective_id=0, has_side_effects=True, vmem_limit_bytes=63 << 20
+            collective_id=0, has_side_effects=True, vmem_limit_bytes=56_200_000
         ),
         name="block",
     )(

time: 70.5 us -> 69 us (0.979)
  local copies, waits for them, and re-layouts: 1.62 us -> 0.68 us
    unnamed x1, local copies, waits for them, and re-layouts: 1.62 us -> 0.68 us
where the time goes in v3:
time: 69 us
  Pallas kernels  67.6 us (98%)
    pallas_call x1, Pallas kernels, per_device(): pl.pallas_call(kernel, out_shape=jax.ShapeDtypeStruct((SHARD, D), BF16),...  67.6 us

profile of v3, /device:TPU:16, one launch (start us, length us, event | category | flops | bytes accessed | tf_op | source)
XLA Modules:
  0.0 69.0 jit_solution(15087912105996752967)
XLA Ops:
  0.7 67.6 %block.1 = bf16[24,4096]{1,0:T(8,128)(2,1)S(1)} custom-call(s32[1]{0:T(128)S(6)} %copy.10.plen_ref, bf16[24,4096]{1,0:T(8,128)(2,1)} %res_hbm.1, bf16[4,96,4096]{2,1,0:T(8,128)(2,1)} %bitcast.3, bf16[4096,512]{1,0:T(8,128)(2,1)} %wq_hbm.1, bf16[64,4096]{1,0:T(8,128)(2,1)} %bitcast.4, bf16[64,4096]{1,0:T(8,128)(2,1)} %bitcast.5, bf16[512,4096]{1,0:T(8,128)(2,1)} %wo_hbm.1, ...), custom_call_target="tpu_custom_call" | custom-call | tf_op jit(solution)/shard_map/block/pallas_call | solution.py:451
  68.3 0.7 copy.11

commit v4 on v3

--- a/solution.py
+++ b/solution.py
@@ -25,7 +25,7 @@
 Z_ORDER = (1, 3, 2)
 GB, GP = 768, 2
 GW = (D - GB) // GP
-SB, CW, PAIRS, AHEAD, BEHIND = 512, 256, 7, 3, 2
+SB, CW, PAIRS, AHEAD, BEHIND = 512, 256, 7, 4, 2
 NC, PW = 2 * PAIRS, 2 * CW
 B1, B2 = PAIRS - 1, PAIRS
 FAR, PLUS, MINUS, OWN = range(4)
@@ -244,13 +244,14 @@
     bx_copy(XP, xf, 2).wait_recv()
     for j in Z_ORDER:
         started(bz_copy(xf, j))
-    each(pass_on, 2)
     for load in loads[3:5]:
         load.wait()
     project(x, GB, D - GB, first=True)
-    each(pass_on, 3)
-    project(xm, GB, D - GB, first=True)
-    project(xp, GB, D - GB, first=True)
+    each(pass_on, 2)
+    for p in range(GP):
+        level(NZ - 1, functools.partial(pass_on, p))
+        project(xm, GB + p * GW, GW, first=p == 0)
+        project(xp, GB + p * GW, GW, first=p == 0)
     for xs in (x, xm, xp, xf):
         for j in range(1, NZ):
             bz_copy(xs, 1, source=j).wait_recv()
@@ -383,7 +384,7 @@
         pl.when(i < PAIRS)(lambda: send_near(i))
         pl.when(i >= BEHIND)(lambda: send_z(i - BEHIND))
 
-        @pl.when(i == 1)
+        @pl.when(i == 4)
         def _():
             for copy, when in sends:
                 copy.wait_send() if when is None else pl.when(when)(copy.wait_send)
@@ -415,13 +416,6 @@
             rn_copy(XP).start()
             rn_copy(XM).start()
 
-    remote(fs, fr, f_send.at[0], f_recv.at[0], neighbour(XP)).wait_send()
-    remote(ns, nr, n_send.at[0], n_recv.at[0, 0], neighbour(XP)).wait_send()
-    for j in range(1, NZ):
-        rz_copy(j).wait_send()
-    for way in (XP, XM):
-        rf_copy(way).wait_send()
-
     @pl.loop(0, PAIRS)
     def _(i):
         mine = own[i].reshape(NZ, SHARD, PW)
@@ -437,6 +431,12 @@
     out_ref[:, :SB] = (
         res_v[:, :SB].astype(F32) + bsum[OWN] + bnr[0].astype(F32) + bnr[1].astype(F32)
     ).astype(BF16)
+    remote(fs, fr, f_send.at[0], f_recv.at[0], neighbour(XP)).wait_send()
+    remote(ns, nr, n_send.at[0], n_recv.at[0, 0], neighbour(XP)).wait_send()
+    for j in range(1, NZ):
+        rz_copy(j).wait_send()
+    for way in (XP, XM):
+        rf_copy(way).wait_send()
     rn_copy(XP).wait_send()
     rn_copy(XM).wait_send()
     sent = zs.at[:, 1:]

time: 69 us -> 68.4 us (level)
  no operation moved by 1% of the time
where the time goes in v4:
time: 68.4 us; the launch traced here: 68.3 us
  Pallas kernels  67 us (98%)
    pallas_call x1, Pallas kernels, per_device(): pl.pallas_call(kernel, out_shape=jax.ShapeDtypeStruct((SHARD, D), BF16),...  67 us

profile of v4, /device:TPU:16, one launch (start us, length us, event | category | flops | bytes accessed | tf_op | source)
XLA Modules:
  0.0 68.3 jit_solution(7085952859881853327)
XLA Ops:
  0.7 67.0 %block.1 = bf16[24,4096]{1,0:T(8,128)(2,1)S(1)} custom-call(s32[1]{0:T(128)S(6)} %copy.10.plen_ref, bf16[24,4096]{1,0:T(8,128)(2,1)} %res_hbm.1, bf16[4,96,4096]{2,1,0:T(8,128)(2,1)} %bitcast.3, bf16[4096,512]{1,0:T(8,128)(2,1)} %wq_hbm.1, bf16[64,4096]{1,0:T(8,128)(2,1)} %bitcast.4, bf16[64,4096]{1,0:T(8,128)(2,1)} %bitcast.5, bf16[512,4096]{1,0:T(8,128)(2,1)} %wo_hbm.1, ...), custom_call_target="tpu_custom_call" | custom-call | tf_op jit(solution)/shard_map/block/pallas_call | solution.py:451
  67.6 0.7 copy.11

commit v5 on v4

--- a/solution.py
+++ b/solution.py
@@ -226,8 +226,9 @@
         rows = pl.ds(pl.multiple_of(i * QW, QW), QW)
         w_v[rows, QW:] = wkv_v[:, rows].astype(F32).T.astype(BF16)
 
-    each(spread, 1)
-    each(pass_on, 0)
+    for p in range(GP):
+        level(1, functools.partial(spread, p))
+        level(0, functools.partial(pass_on, p))
     each(spread, 2)
     for j in Z_ORDER:
         started(bz_copy(x, j))

time: 68.4 us -> 68.4 us (level)
  no operation moved by 1% of the time
where the time goes in v5:
time: 68.4 us; the launch traced here: 68.3 us
  Pallas kernels  67 us (98%)
    pallas_call x1, Pallas kernels, per_device(): pl.pallas_call(kernel, out_shape=jax.ShapeDtypeStruct((SHARD, D), BF16),...  67 us

profile of v5, /device:TPU:16, one launch (start us, length us, event | category | flops | bytes accessed | tf_op | source)
XLA Modules:
  0.0 68.3 jit_solution(5235404214916352289)
XLA Ops:
  0.7 67.0 %block.1 = bf16[24,4096]{1,0:T(8,128)(2,1)S(1)} custom-call(s32[1]{0:T(128)S(6)} %copy.10.plen_ref, bf16[24,4096]{1,0:T(8,128)(2,1)} %res_hbm.1, bf16[4,96,4096]{2,1,0:T(8,128)(2,1)} %bitcast.3, bf16[4096,512]{1,0:T(8,128)(2,1)} %wq_hbm.1, bf16[64,4096]{1,0:T(8,128)(2,1)} %bitcast.4, bf16[64,4096]{1,0:T(8,128)(2,1)} %bitcast.5, bf16[512,4096]{1,0:T(8,128)(2,1)} %wo_hbm.1, ...), custom_call_target="tpu_custom_call" | custom-call | tf_op jit(solution)/shard_map/block/pallas_call | solution.py:452
  67.6 0.7 copy.11
